TPU v7x, 768 devices: a whole 4x8x12 slice. The times are simulated.
768 devices in a mesh: orb: 8 (over y), grp: 48 (over x, z), aux: 2 (over core).
Axes of the slice: x: 4, y: 8, z: 12, core: 2. Of those that a mesh axis runs over, the one named last changes fastest.
Arguments:
- tiles: bfloat16 [18432, 128, 128], P(('orb', 'grp'), 'aux'), may hold values from -6 to 6
- tile_owner: int32 [18432, 1], P(('orb', 'grp')), may hold values from 0 to 47; in each aligned block of 48 rows (0 to 47, 48 to 95, ...) at most 2 rows name the same one
- tile_panel: int32 [18432], P(('orb', 'grp')), may hold values from 0 to 31
- tile_row: int32 [18432], P(('orb', 'grp')), may hold values from 0 to 11
- density: bfloat16 [32, 48, 128, 128], P('orb', 'grp', 'aux'), may hold values from -0.5 to 0.5
Outputs:
- contracted: float32 [4608, 128, 128], P(('orb', 'grp'), 'aux')
Inputs may be any that keep to these rules, and one draw needn't show every extreme that they name: `tile_owner`: in each aligned block of 48 rows (the blocks of one device) no owner appears more than 2 times, and some owner appears exactly 2 times.
All inputs are finite; a program needn't handle non-finite values.
Results may differ from a plain program's by a relative error of at most 0.0029.
Values may be sent and summed in bfloat16 or wider, within the bound.
No kernel may reach another device: no remote copies, remote signals or barrier semaphores. Data moves between devices by JAX's collectives and lax.ppermute only.
A program may use at most 32 MiB of HBM per device.

v0:
```python
import jax
import jax.numpy as jnp
from jax import lax
from jax.sharding import PartitionSpec as P


def shards(tiles, tile_owner, tile_panel, tile_row, density):
    group_size = lax.axis_size("grp")
    tile_count, inner_local, block_size = tiles.shape
    slot_cap = 2 * ((tile_count + 2 * group_size - 1) // (2 * group_size))
    rows_local = tile_count // 4
    owners = tile_owner[:, 0]
    dest_hot = (owners[:, None] == jnp.arange(group_size, dtype=jnp.int32)[None, :]).astype(
        jnp.int32
    )
    slot_rank = jnp.sum((jnp.cumsum(dest_hot, axis=0) - dest_hot) * dest_hot, axis=1)
    place_id = owners * slot_cap + slot_rank
    select = place_id[None, :] == jnp.arange(group_size * slot_cap, dtype=jnp.int32)[:, None]
    row_picker = (tile_row[None, :] == jnp.arange(rows_local, dtype=jnp.int32)[:, None]).astype(
        jnp.float32
    )
    panels = lax.all_gather(density, "orb", axis=0, tiled=True)[:, 0]
    outbound = jnp.dot(
        select.astype(jnp.bfloat16),
        tiles.reshape(tile_count, inner_local * block_size),
        preferred_element_type=jnp.float32,
    )
    outbound = outbound.astype(jnp.bfloat16).reshape(group_size, slot_cap, inner_local, block_size)
    labels = jnp.dot(select.astype(jnp.float32), (tile_panel + 1).astype(jnp.float32))
    labels = labels.astype(jnp.bfloat16).reshape(group_size, slot_cap, 1, 1)
    received, labels = (
        lax.all_to_all(outbound, "grp", split_axis=0, concat_axis=0, tiled=True),
        lax.all_to_all(labels, "grp", split_axis=0, concat_axis=0, tiled=True),
    )
    panel_index = jnp.maximum(labels.reshape(-1).astype(jnp.int32) - 1, 0)
    chosen = jnp.take(panels, panel_index, axis=0)
    stacked = received.reshape(-1, received.shape[2], received.shape[3])
    products = jnp.einsum("ski,skj->sij", stacked, chosen, preferred_element_type=jnp.float32)
    returned = lax.psum_scatter(products, "aux", scatter_dimension=1, tiled=True).astype(
        jnp.bfloat16
    )
    returned = returned.reshape(group_size, -1, returned.shape[1], returned.shape[2])
    returned = lax.all_to_all(returned, "grp", split_axis=0, concat_axis=0, tiled=True)
    row_count = returned.shape[2]
    col_count = returned.shape[3]
    combined = jnp.dot(row_picker, select.T.astype(jnp.float32)).astype(jnp.bfloat16)
    contracted = jnp.dot(
        combined,
        returned.reshape(group_size * slot_cap, row_count * col_count),
        preferred_element_type=jnp.float32,
    )
    return contracted.reshape(rows_local, row_count, col_count)


def solution(mesh):
    return jax.shard_map(
        shards,
        mesh=mesh,
        in_specs=(
            P(("orb", "grp"), "aux", None),
            P(("orb", "grp"), None),
            P(("orb", "grp")),
            P(("orb", "grp")),
            P("orb", "grp", "aux", None),
        ),
        out_specs=P(("orb", "grp"), "aux", None),
        check_vma=False,
    )
```

profile of v0, /device:TPU:1, one launch (start us, length us, event | category | flops | bytes accessed | tf_op | source)
XLA Modules:
  0.0 209.1 jit_solution(18115015010018792132)
XLA Ops:
  6.5 0.7 fusion.16
  7.3 0.1 reduce_window_sum.11
  7.3 0.8 select_reduce_fusion
  8.2 0.7 multiply_add_fusion
  8.8 0.8 fusion.8
  9.6 0.8 reshape.82
  10.4 18.8 %all-to-all-start.1 = ((bf16[48,2,1,1]{1,3,2,0:T(2,128)(2,1)}), bf16[48,2,1,1]{1,3,2,0:T(2,128)(2,1)S(1)}, u32[]{:S(2)}, u32[]{:S(2)}) async-start(bf16[48,2,1,1]{1,3,2,0:T(2,128)(2,1)} %reshape.82), calls=%async_computation.1 | async-start | bytes 49152 | tf_op jit(solution)/shard_map/all_to_all | solution.py:33
  29.3 1.8 fusion.6
  31.0 1.6 copy.14
  32.6 7.7 %all-to-all-done.1 = bf16[48,2,1,1]{1,3,2,0:T(2,128)(2,1)S(1)} async-done(((bf16[48,2,1,1]{1,3,2,0:T(2,128)(2,1)}), bf16[48,2,1,1]{1,3,2,0:T(2,128)(2,1)S(1)}, u32[]{:S(2)}, u32[]{:S(2)}) %all-to-all-start.1) | async-done | bytes 224 | tf_op jit(solution)/shard_map/all_to_all | solution.py:33
  40.3 0.0 copy-start
  40.3 4.7 %all-to-all-start = ((bf16[48,2,64,128]{3,2,1,0:T(8,128)(2,1)}), bf16[48,2,64,128]{3,2,1,0:T(8,128)(2,1)S(1)}, u32[]{:S(2)}, u32[]{:S(2)}) async-start(bf16[48,2,64,128]{3,2,1,0:T(8,128)(2,1)} %bitcast.14), calls=%async_computation | async-start | bytes 3145728 | tf_op jit(solution)/shard_map/all_to_all | solution.py:32
  45.0 0.0 reduce-scatter.2.cloned.1.call-start
  45.1 0.0 copy-done
  45.1 22.5 %all_gather.3 = bf16[32,1,64,128]{3,2,1,0:T(8,128)(2,1)S(1)} all-gather(bf16[4,1,64,128]{3,2,1,0:T(8,128)(2,1)S(1)} %copy-done), channel_id=1, replica_groups=mesh['orb'=8,'grp'=48,'aux'=2] {'orb'}, dimensions={0}, use_global_device_ids=true | all-gather | bytes 589824 | tf_op jit(solution)/shard_map/all_gather | solution.py:22
  67.6 0.1 compare_reduce_fusion
  67.7 0.1 le.16
  67.8 0.1 fusion.19
  67.9 0.1 reshape.72
  68.1 1.9 gather_fusion
  70.0 26.9 %all-to-all-done = bf16[48,2,64,128]{3,2,1,0:T(8,128)(2,1)S(1)} async-done(((bf16[48,2,64,128]{3,2,1,0:T(8,128)(2,1)}), bf16[48,2,64,128]{3,2,1,0:T(8,128)(2,1)S(1)}, u32[]{:S(2)}, u32[]{:S(2)}) %all-to-all-start) | async-done | bytes 1572896 | tf_op jit(solution)/shard_map/all_to_all | solution.py:32
  96.9 5.3 %fusion.3 = f32[96,128,128]{2,1,0:T(8,128)} fusion(bf16[96,64,128]{2,1,0:T(8,128)(2,1)S(1)} %bitcast.40, bf16[96,64,128]{2,1,0:T(8,128)(2,1)} %gather_fusion, pred[96]{0:T(512)(128)(4,1)S(1)} %le.16), kind=kOutput, calls=%fused_computation.6 | convolution fusion | flops 202113024 | bytes 9437280 | tf_op jit(solution)/shard_map/ski,skj->sij/dot_general | solution.py:38
  102.1 0.0 reduce-scatter.2.cloned.1.call-update
  102.2 28.9 %reduce-scatter.2.cloned.1.call-done = f32[96,64,128]{2,1,0:T(8,128)} async-done(((f32[96,128,128]{2,1,0:T(8,128)}), f32[96,64,128]{2,1,0:T(8,128)}) %reduce-scatter.2.cloned.1.call-update) | async-done | bytes 3145744 | tf_op jit(solution)/shard_map/reduce_scatter | solution.py:39
  131.0 2.2 %convert_element_type.42 = bf16[96,64,128]{2,1,0:T(8,128)(2,1)S(1)} convert(f32[96,64,128]{2,1,0:T(8,128)} %reduce-scatter.2.cloned.1.call-done) | non-fusion elementwise | flops 786432 | bytes 4718592 | tf_op jit(solution)/shard_map/convert_element_type | solution.py:39
  133.3 0.0 copy-start.1
  133.3 67.1 %all_to_all.15 = bf16[48,2,64,128]{3,2,1,0:T(8,128)(2,1)S(1)} all-to-all(bf16[48,2,64,128]{3,2,1,0:T(8,128)(2,1)S(1)} %bitcast.41), channel_id=1, replica_groups=mesh['orb'=8,'grp'=48,'aux'=2] {'grp'}, dimensions={0} | all-to-all | bytes 3145728 | tf_op jit(solution)/shard_map/all_to_all | solution.py:43
  200.3 0.0 copy-done.1
  200.4 1.0 fusion
  201.3 0.9 copy.11
  (1 shorter events, 0.0 us)
Async XLA Ops:
  10.4 29.9 %all-to-all-start.1 = ((bf16[48,2,1,1]{1,3,2,0:T(2,128)(2,1)}), bf16[48,2,1,1]{1,3,2,0:T(2,128)(2,1)S(1)}, u32[]{:S(2)}, u32[]{:S(2)}) async-start(bf16[48,2,1,1]{1,3,2,0:T(2,128)(2,1)} %reshape.82), calls=%async_computation.1 | async-start | bytes 49152 | tf_op jit(solution)/shard_map/all_to_all | solution.py:33
  40.3 4.8 %copy-start = (bf16[4,1,64,128]{3,2,1,0:T(8,128)(2,1)S(1)}, bf16[4,1,64,128]{3,2,1,0:T(8,128)(2,1)}, u32[]{:S(2)}) copy-start(bf16[4,1,64,128]{3,2,1,0:T(8,128)(2,1)} %param.9) | copy-start | bytes 196612
  40.3 56.6 %all-to-all-start = ((bf16[48,2,64,128]{3,2,1,0:T(8,128)(2,1)}), bf16[48,2,64,128]{3,2,1,0:T(8,128)(2,1)S(1)}, u32[]{:S(2)}, u32[]{:S(2)}) async-start(bf16[48,2,64,128]{3,2,1,0:T(8,128)(2,1)} %bitcast.14), calls=%async_computation | async-start | bytes 3145728 | tf_op jit(solution)/shard_map/all_to_all | solution.py:32
  45.0 86.0 %reduce-scatter.2.cloned.1.call-start = ((), (), s32[]{:S(2)}) async-start(), calls=%async_computation.4 | async-start | bytes 9437184 | tf_op jit(solution)/shard_map/reduce_scatter | solution.py:39
  133.3 67.1 %copy-start.1 = (s32[48]{0:T(128)S(1)}, s32[48]{0:T(128)}, u32[]{:S(2)}) copy-start(s32[48]{0:T(128)} %param.8) | copy-start | bytes 580
Sparse Core Ops, SparseCore 0:
  102.3 28.6 reduce-scatter.1
where the time goes:
time: 212 us; the launch traced here: 209 us
  blocking collectives  89.6 us (42%)
  waiting for transfers between devices  63.4 us (30%)
  starting transfers between devices  23.6 us (11%)
  between operations  13.5 us (6%)
  matrix products  8.82 us (4%)
  local copies, waits for them, and re-layouts  5.43 us (3%)
  other arithmetic  4.77 us (2%)
    all_to_all x1, blocking collectives, shards(): lax.all_to_all(returned, 'grp', split_axis=0, concat_axis=0, tiled=True)  67.1 us
    reduce_scatter x1, waiting for transfers between devices, shards(): lax.psum_scatter(products, 'aux', scatter_dimension=1, tiled=True)  28.9 us
    all_to_all x1, waiting for transfers between devices, shards(): lax.all_to_all(outbound, 'grp', split_axis=0, concat_axis=0, tiled=True)  26.9 us
    all_gather x1, blocking collectives, shards(): panels = lax.all_gather(density, 'orb', axis=0, tiled=True)[:, 0]  22.5 us
    all_to_all x1, starting transfers between devices, shards(): lax.all_to_all(labels, 'grp', split_axis=0, concat_axis=0, tiled=True)  18.8 us
    all_to_all x1, waiting for transfers between devices, shards(): lax.all_to_all(labels, 'grp', split_axis=0, concat_axis=0, tiled=True)  7.68 us
    dot_general x1, matrix products, shards(): jnp.einsum('ski,skj->sij', stacked, chosen, preferred_element_type=jnp.fl...  5.26 us
    all_to_all x1, starting transfers between devices, shards(): lax.all_to_all(outbound, 'grp', split_axis=0, concat_axis=0, tiled=True)  4.73 us
  transfers between devices with their start and end apart: 3, of which 3 were waited for; matrix products, arithmetic and copies ran while one was open for 3% of the time, Pallas kernels for 0%

commit v1 on v0

v1 whole, which is shorter than its diff:
```python
import functools

import jax
import jax.numpy as jnp
from jax import lax
from jax.experimental import pallas as pl
from jax.experimental.pallas import tpu as pltpu
from jax.sharding import Mesh, PartitionSpec as P

Z = 12
PLANE = ("orb", "x")


def pick_kernel(index_ref, table_ref, out_ref):
    def body(i, carry):
        out_ref[i] = table_ref[index_ref[i]]
        return carry

    lax.fori_loop(0, out_ref.shape[0], body, 0, unroll=32)


def sum_kernel(row_ref, core_ref, tiles_ref, panels_ref, out_ref):
    core = core_ref[0]
    half = out_ref.shape[2]
    out_ref[...] = jnp.zeros_like(out_ref)
    for t in range(tiles_ref.shape[0]):
        product = lax.dot_general(
            tiles_ref[t], panels_ref[t], (((0,), (0,)), ((), ())), preferred_element_type=jnp.float32
        )
        row = row_ref[t]
        out_ref[core, row] += product[:half]
        out_ref[1 - core, row] += product[half:]


def shards(tiles, tile_owner, tile_panel, tile_row, density):
    plane = lax.axis_size(PLANE)
    orbs, xs = lax.axis_size("orb"), lax.axis_size("x")
    count, inner, block = tiles.shape
    held = density.shape[0]
    part = inner // plane
    rows_local = count // 4
    owners = tile_owner[:, 0]
    high = (owners % Z) * orbs + tile_panel // held
    low = (owners // Z) * held + tile_panel % held
    asked = jnp.pad(jnp.stack([high, low]).astype(jnp.bfloat16), ((0, 6), (0, 128 - count)))
    slices = density.reshape(held, plane, part, block).transpose(1, 0, 2, 3).reshape(plane, held * part, block)
    outbound = jnp.concatenate([slices, jnp.broadcast_to(asked[None], (plane, 8, 128))], axis=1)
    inbound = lax.all_to_all(outbound, PLANE, 0, 0, tiled=True)
    wanted = inbound[:, held * part : held * part + 2, :count].astype(jnp.int32)
    index = (wanted[:, 0] * (xs * held) + wanted[:, 1]).reshape(-1)
    mine = inbound[:, : held * part]
    table = lax.all_to_all(
        jnp.broadcast_to(mine[None], (Z,) + mine.shape), "z", 0, 0, tiled=True
    )
    picked = pl.pallas_call(
        pick_kernel,
        out_shape=jax.ShapeDtypeStruct((plane * count, part, block), jnp.bfloat16),
        in_specs=[pl.BlockSpec(memory_space=pltpu.SMEM), pl.BlockSpec(memory_space=pltpu.VMEM)],
        out_specs=pl.BlockSpec(memory_space=pltpu.VMEM),
        compiler_params=pltpu.CompilerParams(vmem_limit_bytes=48 * 1024 * 1024),
    )(index, table.reshape(Z * plane * held, part, block))
    panels = lax.all_to_all(picked.reshape(plane, count * part, block), PLANE, 0, 0, tiled=True)
    panels = panels.reshape(plane, count, part, block).transpose(1, 0, 2, 3).reshape(count, inner, block)
    core = lax.axis_index("aux").reshape(1)
    summed = pl.pallas_call(
        sum_kernel,
        out_shape=jax.ShapeDtypeStruct((2, rows_local, block // 2, block), jnp.float32),
        in_specs=[pl.BlockSpec(memory_space=pltpu.SMEM)] * 2 + [pl.BlockSpec(memory_space=pltpu.VMEM)] * 2,
        out_specs=pl.BlockSpec(memory_space=pltpu.VMEM),
        compiler_params=pltpu.CompilerParams(vmem_limit_bytes=48 * 1024 * 1024),
    )(tile_row, core, tiles, panels)
    other = lax.ppermute(summed[1], "aux", [(0, 1), (1, 0)])
    return summed[0] + other


def solution(mesh):
    orbs, grps, cores = mesh.devices.shape
    split = Mesh(mesh.devices.reshape(orbs, grps // Z, Z, cores), ("orb", "x", "z", "aux"))
    own = ("orb", "x", "z")
    return jax.shard_map(
        shards,
        mesh=split,
        in_specs=(
            P(own, "aux", None),
            P(own, None),
            P(own),
            P(own),
            P("orb", ("x", "z"), "aux", None),
        ),
        out_specs=P(own, "aux", None),
        check_vma=False,
    )
```

time: 212 us -> 105 us (0.50)
  the two profiles are of different devices: /device:TPU:1 before, /device:TPU:65 now
where the time goes in v1:
time: 105 us
  waiting for transfers between devices  53.8 us (51%)
  starting transfers between devices  23.1 us (22%)
  blocking collectives  18.8 us (18%)
  Pallas kernels  4.28 us (4%)
  local copies, waits for them, and re-layouts  3.87 us (4%)
    all_to_all x1, waiting for transfers between devices, shards(): lax.all_to_all(jnp.broadcast_to(mine[None], (Z,) + mine.shape), 'z', 0, 0...  31.8 us
    all_to_all x1, waiting for transfers between devices, shards(): lax.all_to_all(picked.reshape(plane, count * part, block), PLANE, 0, 0, t...  20.6 us
    all_to_all x1, blocking collectives, shards(): inbound = lax.all_to_all(outbound, PLANE, 0, 0, tiled=True)  18.8 us
    all_to_all x1, starting transfers between devices, shards(): lax.all_to_all(jnp.broadcast_to(mine[None], (Z,) + mine.shape), 'z', 0, 0...  14.2 us
    ppermute x1, starting transfers between devices, shards(): other = lax.ppermute(summed[1], 'aux', [(0, 1), (1, 0)])  5 us
    all_to_all x1, starting transfers between devices, shards(): lax.all_to_all(picked.reshape(plane, count * part, block), PLANE, 0, 0, t...  3.91 us
    pallas_call x1, Pallas kernels, shards(): pl.pallas_call(pick_kernel, out_shape=jax.ShapeDtypeStruct((plane * count...  2.95 us
  transfers between devices with their start and end apart: 3, of which 3 were waited for; matrix products, arithmetic and copies ran while one was open for 0% of the time, Pallas kernels for 0%

profile of v1, /device:TPU:65, one launch (start us, length us, event | category | flops | bytes accessed | tf_op | source)
XLA Modules:
  0.0 104.9 jit_solution(12442226248645632153)
XLA Ops:
  0.0 0.0 copy-start.2
  0.0 0.0 copy-start.3
  0.0 0.9 copy.13
  0.9 0.0 copy-done.2
  0.9 0.0 copy-done.3
  1.0 0.1 copy.14
  1.0 18.8 %all_to_all.15 = bf16[32,16,128]{2,1,0:T(8,128)(2,1)S(1)} all-to-all(bf16[32,16,128]{2,1,0:T(8,128)(2,1)S(1)} %copy.14), channel_id=1, replica_groups=mesh['orb'=8,'x'=4,'z'=12,'aux'=2] {'orb','x'}, dimensions={0} | all-to-all | bytes 262144 | tf_op jit(solution)/shard_map/all_to_all | solution.py:48
  19.9 1.0 broadcast_in_dim.5
  20.9 14.2 %all-to-all-start.1 = ((bf16[12,32,8,128]{3,2,1,0:T(8,128)(2,1)}), bf16[12,32,8,128]{3,2,1,0:T(8,128)(2,1)S(1)}, u32[]{:S(2)}, u32[]{:S(2)}) async-start(bf16[12,32,8,128]{3,2,1,0:T(8,128)(2,1)} %broadcast_in_dim.5), calls=%async_computation.1 | async-start | bytes 1572864 | tf_op jit(solution)/shard_map/all_to_all | solution.py:52
  35.1 0.1 fusion.1
  35.2 0.1 add.35.index_ref
  35.3 31.8 %all-to-all-done.1 = bf16[12,32,8,128]{3,2,1,0:T(8,128)(2,1)S(1)} async-done(((bf16[12,32,8,128]{3,2,1,0:T(8,128)(2,1)}), bf16[12,32,8,128]{3,2,1,0:T(8,128)(2,1)S(1)}, u32[]{:S(2)}, u32[]{:S(2)}) %all-to-all-start.1) | async-done | bytes 786464 | tf_op jit(solution)/shard_map/all_to_all | solution.py:52
  67.1 3.0 %shard_map.55 = bf16[1536,2,128]{2,1,0:T(2,128)(2,1)} custom-call(s32[1536]{0:T(1024)S(1)} %add.35.index_ref, bf16[1536,2,128]{2,1,0:T(2,128)(2,1)S(1)} %bitcast.44), custom_call_target="tpu_custom_call" | custom-call | tf_op jit(solution)/shard_map/pallas_call | solution.py:55
  70.1 3.9 %all-to-all-start.2 = ((bf16[32,96,128]{2,1,0:T(8,128)(2,1)}), bf16[32,96,128]{2,1,0:T(8,128)(2,1)S(1)}, u32[]{:S(2)}, u32[]{:S(2)}) async-start(bf16[32,96,128]{2,1,0:T(8,128)(2,1)} %bitcast.10), calls=%async_computation.2 | async-start | bytes 1572864 | tf_op jit(solution)/shard_map/all_to_all | solution.py:62
  74.0 20.6 %all-to-all-done.2 = bf16[32,96,128]{2,1,0:T(8,128)(2,1)S(1)} async-done(((bf16[32,96,128]{2,1,0:T(8,128)(2,1)}), bf16[32,96,128]{2,1,0:T(8,128)(2,1)S(1)}, u32[]{:S(2)}, u32[]{:S(2)}) %all-to-all-start.2) | async-done | bytes 786464 | tf_op jit(solution)/shard_map/all_to_all | solution.py:62
  94.6 0.3 copy.15
  94.9 0.0 copy-start
  94.9 0.8 copy.16
  95.7 0.0 copy-start.1
  95.7 0.3 copy-done
  96.0 0.4 copy-done.1
  96.4 1.3 %shard_map.56 = f32[2,12,64,128]{3,2,1,0:T(8,128)S(1)} custom-call(s32[48]{0:T(128)S(1)} %copy-done.1, s32[1]{0:T(128)} %bitcast.core_ref, bf16[48,64,128]{2,1,0:T(8,128)(2,1)S(1)} %copy-done, bf16[48,64,128]{2,1,0:T(8,128)(2,1)S(1)} %bitcast.45), custom_call_target="tpu_custom_call" | custom-call | tf_op jit(solution)/shard_map/pallas_call | solution.py:65
  97.8 5.0 %collective-permute-start = (f32[12,64,128]{2,1,0:T(8,128)S(1)}, f32[12,64,128]{2,1,0:T(8,128)S(1)}, u32[]{:S(2)}, u32[]{:S(2)}) collective-permute-start(f32[12,64,128]{2,1,0:T(8,128)S(1)} %slice_bitcast_fusion), channel_id=1, source_target_pairs={{0,1},{1,0},{2,3},{3,2},{4,5},{5,4},{6,7},{7,6},{8,9},{9,8},{10,11... | collective-permute-start | bytes 1179656 | tf_op jit(solution)/shard_map/ppermute | solution.py:72
  102.8 1.3 %collective-permute-done = f32[12,64,128]{2,1,0:T(8,128)S(1)} collective-permute-done((f32[12,64,128]{2,1,0:T(8,128)S(1)}, f32[12,64,128]{2,1,0:T(8,128)S(1)}, u32[]{:S(2)}, u32[]{:S(2)}) %collective-permute-start) | collective-permute-done | bytes 393248 | tf_op jit(solution)/shard_map/ppermute | solution.py:72
  104.1 0.8 fusion
  (7 shorter events, 0.1 us)
Async XLA Ops:
  0.0 0.9 copy-start.2
  0.0 0.9 copy-start.3
  20.9 46.2 %all-to-all-start.1 = ((bf16[12,32,8,128]{3,2,1,0:T(8,128)(2,1)}), bf16[12,32,8,128]{3,2,1,0:T(8,128)(2,1)S(1)}, u32[]{:S(2)}, u32[]{:S(2)}) async-start(bf16[12,32,8,128]{3,2,1,0:T(8,128)(2,1)} %broadcast_in_dim.5), calls=%async_computation.1 | async-start | bytes 1572864 | tf_op jit(solution)/shard_map/all_to_all | solution.py:52
  70.1 24.5 %all-to-all-start.2 = ((bf16[32,96,128]{2,1,0:T(8,128)(2,1)}), bf16[32,96,128]{2,1,0:T(8,128)(2,1)S(1)}, u32[]{:S(2)}, u32[]{:S(2)}) async-start(bf16[32,96,128]{2,1,0:T(8,128)(2,1)} %bitcast.10), calls=%async_computation.2 | async-start | bytes 1572864 | tf_op jit(solution)/shard_map/all_to_all | solution.py:62
  94.9 1.1 %copy-start = (bf16[48,64,128]{2,1,0:T(8,128)(2,1)S(1)}, bf16[48,64,128]{2,1,0:T(8,128)(2,1)}, u32[]{:S(2)}) copy-start(bf16[48,64,128]{2,1,0:T(8,128)(2,1)} %tiles_ref.1) | copy-start | bytes 2359300
  95.7 0.7 copy-start.1
  97.8 6.3 %collective-permute-start = (f32[12,64,128]{2,1,0:T(8,128)S(1)}, f32[12,64,128]{2,1,0:T(8,128)S(1)}, u32[]{:S(2)}, u32[]{:S(2)}) collective-permute-start(f32[12,64,128]{2,1,0:T(8,128)S(1)} %slice_bitcast_fusion), channel_id=1, source_target_pairs={{0,1},{1,0},{2,3},{3,2},{4,5},{5,4},{6,7},{7,6},{8,9},{9,8},{10,11... | collective-permute-start | bytes 1179656 | tf_op jit(solution)/shard_map/ppermute | solution.py:72

commit v2 on v1

--- a/solution.py
+++ b/solution.py
@@ -49,9 +49,7 @@
     wanted = inbound[:, held * part : held * part + 2, :count].astype(jnp.int32)
     index = (wanted[:, 0] * (xs * held) + wanted[:, 1]).reshape(-1)
     mine = inbound[:, : held * part]
-    table = lax.all_to_all(
-        jnp.broadcast_to(mine[None], (Z,) + mine.shape), "z", 0, 0, tiled=True
-    )
+    table = lax.all_gather(mine, "z", axis=0, tiled=False)
     picked = pl.pallas_call(
         pick_kernel,
         out_shape=jax.ShapeDtypeStruct((plane * count, part, block), jnp.bfloat16),

time: 105 us -> 91.6 us (0.87)
  the two profiles are of different devices: /device:TPU:65 before, /device:TPU:1 now
where the time goes in v2:
time: 91.6 us; the launch traced here: 91.3 us
  blocking collectives  51.4 us (56%)
  waiting for transfers between devices  16.5 us (18%)
  starting transfers between devices  15.2 us (17%)
  Pallas kernels  4.29 us (5%)
  local copies, waits for them, and re-layouts  2.84 us (3%)
  other arithmetic  0.93 us (1%)
    all_gather x1, blocking collectives, shards(): table = lax.all_gather(mine, 'z', axis=0, tiled=False)  31.7 us
    all_to_all x1, blocking collectives, shards(): inbound = lax.all_to_all(outbound, PLANE, 0, 0, tiled=True)  19.6 us
    all_to_all x1, waiting for transfers between devices, shards(): lax.all_to_all(picked.reshape(plane, count * part, block), PLANE, 0, 0, t...  15.2 us
    ppermute x1, starting transfers between devices, shards(): other = lax.ppermute(summed[1], 'aux', [(0, 1), (1, 0)])  11.1 us
    all_to_all x1, starting transfers between devices, shards(): lax.all_to_all(picked.reshape(plane, count * part, block), PLANE, 0, 0, t...  4.1 us
    pallas_call x1, Pallas kernels, shards(): pl.pallas_call(pick_kernel, out_shape=jax.ShapeDtypeStruct((plane * count...  2.97 us
  transfers between devices with their start and end apart: 2, of which 2 were waited for; matrix products, arithmetic and copies ran while one was open for 0% of the time, Pallas kernels for 0%

profile of v2, /device:TPU:1, one launch (start us, length us, event | category | flops | bytes accessed | tf_op | source)
XLA Modules:
  0.0 91.3 jit_solution(10823374659555231967)
XLA Ops:
  0.0 0.0 copy-start.2
  0.0 0.0 copy-start.3
  0.0 0.9 copy.10
  0.9 0.0 copy-done.2
  0.9 0.0 copy-done.3
  1.0 19.6 %all_to_all.10 = bf16[32,16,128]{2,1,0:T(8,128)(2,1)S(1)} all-to-all(bf16[32,16,128]{2,1,0:T(8,128)(2,1)S(1)} %pad_maximum_fusion), channel_id=1, replica_groups=mesh['orb'=8,'x'=4,'z'=12,'aux'=2] {'orb','x'}, dimensions={0} | all-to-all | bytes 262144 | tf_op jit(solution)/shard_map/all_to_all | solution.py:48
  20.7 31.7 %all-gather = bf16[384,8,128]{2,1,0:T(8,128)(2,1)S(1)} all-gather(bf16[32,8,128]{2,1,0:T(8,128)(2,1)S(1)} %slice.27), channel_id=2, replica_groups=mesh['orb'=8,'x'=4,'z'=12,'aux'=2] {'z'}, dimensions={0}, use_global_device_ids=true | all-gather | bytes 851968 | tf_op jit(solution)/shard_map/all_gather | solution.py:52
  52.4 0.1 fusion.1
  52.5 0.1 add.35.index_ref
  52.6 3.0 %shard_map.55 = bf16[1536,2,128]{2,1,0:T(2,128)(2,1)} custom-call(s32[1536]{0:T(1024)S(1)} %add.35.index_ref, bf16[1536,2,128]{2,1,0:T(2,128)(2,1)S(1)} %bitcast.44), custom_call_target="tpu_custom_call" | custom-call | tf_op jit(solution)/shard_map/pallas_call | solution.py:53
  55.6 4.1 %all-to-all-start.1 = ((bf16[32,96,128]{2,1,0:T(8,128)(2,1)}), bf16[32,96,128]{2,1,0:T(8,128)(2,1)S(1)}, u32[]{:S(2)}, u32[]{:S(2)}) async-start(bf16[32,96,128]{2,1,0:T(8,128)(2,1)} %bitcast.10), calls=%async_computation.1 | async-start | bytes 1572864 | tf_op jit(solution)/shard_map/all_to_all | solution.py:60
  59.7 15.2 %all-to-all-done.1 = bf16[32,96,128]{2,1,0:T(8,128)(2,1)S(1)} async-done(((bf16[32,96,128]{2,1,0:T(8,128)(2,1)}), bf16[32,96,128]{2,1,0:T(8,128)(2,1)S(1)}, u32[]{:S(2)}, u32[]{:S(2)}) %all-to-all-start.1) | async-done | bytes 786464 | tf_op jit(solution)/shard_map/all_to_all | solution.py:60
  74.9 0.3 copy.11
  75.2 0.0 copy-start
  75.2 0.8 copy.12
  76.0 0.0 copy-start.1
  76.0 0.3 copy-done
  76.3 0.4 copy-done.1
  76.7 1.3 %shard_map.56 = f32[2,12,64,128]{3,2,1,0:T(8,128)S(1)} custom-call(s32[48]{0:T(128)S(1)} %copy-done.1, s32[1]{0:T(128)} %bitcast.core_ref, bf16[48,64,128]{2,1,0:T(8,128)(2,1)S(1)} %copy-done, bf16[48,64,128]{2,1,0:T(8,128)(2,1)S(1)} %bitcast.45), custom_call_target="tpu_custom_call" | custom-call | tf_op jit(solution)/shard_map/pallas_call | solution.py:63
  78.1 11.1 %collective-permute-start = (f32[12,64,128]{2,1,0:T(8,128)S(1)}, f32[12,64,128]{2,1,0:T(8,128)S(1)}, u32[]{:S(2)}, u32[]{:S(2)}) collective-permute-start(f32[12,64,128]{2,1,0:T(8,128)S(1)} %slice_bitcast_fusion), channel_id=1, source_target_pairs={{0,1},{1,0},{2,3},{3,2},{4,5},{5,4},{6,7},{7,6},{8,9},{9,8},{10,11... | collective-permute-start | bytes 1179656 | tf_op jit(solution)/shard_map/ppermute | solution.py:70
  89.2 1.3 %collective-permute-done = f32[12,64,128]{2,1,0:T(8,128)S(1)} collective-permute-done((f32[12,64,128]{2,1,0:T(8,128)S(1)}, f32[12,64,128]{2,1,0:T(8,128)S(1)}, u32[]{:S(2)}, u32[]{:S(2)}) %collective-permute-start) | collective-permute-done | bytes 393248 | tf_op jit(solution)/shard_map/ppermute | solution.py:70
  90.5 0.8 fusion
  (7 shorter events, 0.1 us)
Async XLA Ops:
  0.0 0.9 %copy-start.2 = (s32[48]{0:T(128)S(1)}, s32[48]{0:T(128)}, u32[]{:S(2)}) copy-start(s32[48]{0:T(128)} %param.7) | copy-start | bytes 580
  0.0 0.9 %copy-start.3 = (s32[48,1]{0,1:T(1,128)S(1)}, s32[48,1]{0,1:T(1,128)}, u32[]{:S(2)}) copy-start(s32[48,1]{0,1:T(1,128)} %param.6) | copy-start | bytes 580
  55.6 19.3 %all-to-all-start.1 = ((bf16[32,96,128]{2,1,0:T(8,128)(2,1)}), bf16[32,96,128]{2,1,0:T(8,128)(2,1)S(1)}, u32[]{:S(2)}, u32[]{:S(2)}) async-start(bf16[32,96,128]{2,1,0:T(8,128)(2,1)} %bitcast.10), calls=%async_computation.1 | async-start | bytes 1572864 | tf_op jit(solution)/shard_map/all_to_all | solution.py:60
  75.2 1.1 %copy-start = (bf16[48,64,128]{2,1,0:T(8,128)(2,1)S(1)}, bf16[48,64,128]{2,1,0:T(8,128)(2,1)}, u32[]{:S(2)}) copy-start(bf16[48,64,128]{2,1,0:T(8,128)(2,1)} %tiles_ref.1) | copy-start | bytes 2359300
  76.0 0.7 copy-start.1
  78.1 12.4 %collective-permute-start = (f32[12,64,128]{2,1,0:T(8,128)S(1)}, f32[12,64,128]{2,1,0:T(8,128)S(1)}, u32[]{:S(2)}, u32[]{:S(2)}) collective-permute-start(f32[12,64,128]{2,1,0:T(8,128)S(1)} %slice_bitcast_fusion), channel_id=1, source_target_pairs={{0,1},{1,0},{2,3},{3,2},{4,5},{5,4},{6,7},{7,6},{8,9},{9,8},{10,11... | collective-permute-start | bytes 1179656 | tf_op jit(solution)/shard_map/ppermute | solution.py:70

commit v3 on v2

v3 whole, which is shorter than its diff:
```python
import jax
import jax.numpy as jnp
from jax import lax
from jax.experimental import pallas as pl
from jax.experimental.pallas import tpu as pltpu
from jax.sharding import Mesh, PartitionSpec as P

Z = 12
PLANE = ("orb", "x")


def pick_kernel(index_hbm, table_ref, out_hbm, index_ref, out_ref, in_sem, out_sem):
    pieces = in_sem.shape[0]
    lines, width = index_ref.shape
    per = lines // pieces
    fetches, sends = [], []
    for piece in range(pieces):
        span = pl.ds(piece * per, per)
        fetches.append(pltpu.make_async_copy(index_hbm.at[span], index_ref.at[span], in_sem.at[piece]))
        fetches[-1].start()
    for piece in range(pieces):
        fetches[piece].wait()

        def body(line, carry):
            for i in range(width):
                out_ref[line * width + i] = table_ref[index_ref[line, i]]
            return carry

        lax.fori_loop(piece * per, (piece + 1) * per, body, 0)
        span = pl.ds(piece * per * width, per * width)
        sends.append(pltpu.make_async_copy(out_ref.at[span], out_hbm.at[span], out_sem.at[piece]))
        sends[-1].start()
    for send in sends:
        send.wait()


def turn_kernel(core_ref, row_ref, tiles_ref, sent_ref, kept_ref, near_row_ref):
    half = sent_ref.shape[1]
    first = core_ref[0] == 0
    near_row_ref[...] = row_ref[...]

    def body(t, carry):
        turned = tiles_ref[t].T
        sent_ref[t] = jnp.where(first, turned[half:], turned[:half])
        kept_ref[t] = jnp.where(first, turned[:half], turned[half:])
        return carry

    lax.fori_loop(0, tiles_ref.shape[0], body, 0, unroll=4)


def sum_kernel(row_vmem, turned_ref, panels_ref, out_ref, row_ref, product_ref, row_sem):
    fetch = pltpu.make_async_copy(row_vmem, row_ref, row_sem)
    fetch.start()
    count, _, inner = turned_ref.shape
    out_ref[...] = jnp.zeros_like(out_ref)
    for t in range(count):
        panel = panels_ref[:, t].reshape(inner, out_ref.shape[2])
        product_ref[t] = jnp.dot(turned_ref[t], panel, preferred_element_type=jnp.float32)
    fetch.wait()
    for t in range(count):
        out_ref[row_ref[0, t]] += product_ref[t]


def shards(tiles, tile_owner, tile_panel, tile_row, density):
    plane = lax.axis_size(PLANE)
    xs = lax.axis_size("x")
    count, inner, block = tiles.shape
    held = density.shape[0]
    part = inner // plane
    rows_local = count // 4
    owners = tile_owner[:, 0]
    high = (owners % Z) * lax.axis_size("orb") + tile_panel // held
    low = (owners // Z) * held + tile_panel % held
    asked = jnp.pad(jnp.stack([high, low]).astype(jnp.bfloat16), ((0, 6), (0, block - count)))
    slices = density.reshape(held, plane, part, block).transpose(1, 0, 2, 3).reshape(plane, held * part, block)
    outbound = jnp.concatenate([slices, jnp.broadcast_to(asked[None], (plane, 8, block))], axis=1)
    inbound = lax.all_to_all(outbound, PLANE, 0, 0, tiled=True)
    wanted = inbound[:, held * part : held * part + 2, :count].astype(jnp.int32)
    index = (wanted[:, 0] * (xs * held) + wanted[:, 1]).reshape(-1)
    mine = inbound[:, : held * part]
    table = lax.all_gather(mine, "z", axis=0, tiled=False)
    pieces = 12
    picked = pl.pallas_call(
        pick_kernel,
        out_shape=jax.ShapeDtypeStruct((plane * count, part, block), jnp.bfloat16),
        in_specs=[pl.BlockSpec(memory_space=pl.ANY), pl.BlockSpec(memory_space=pltpu.VMEM)],
        out_specs=pl.BlockSpec(memory_space=pl.ANY),
        scratch_shapes=[
            pltpu.SMEM((plane * count // 128, 128), jnp.int32),
            pltpu.VMEM((plane * count, part, block), jnp.bfloat16),
            pltpu.SemaphoreType.DMA((pieces,)),
            pltpu.SemaphoreType.DMA((pieces,)),
        ],
        compiler_params=pltpu.CompilerParams(vmem_limit_bytes=16 * 1024 * 1024),
    )(index.reshape(-1, 128), table.reshape(Z * plane * held, part, block))
    panels = lax.all_to_all(picked.reshape(plane, count * part, block), PLANE, 0, 0, tiled=True)
    panels = panels.reshape(plane, count, part, block)
    half = block // 2
    core = lax.axis_index("aux").reshape(1)
    sent, kept, near_row = pl.pallas_call(
        turn_kernel,
        out_shape=[jax.ShapeDtypeStruct((count, half, inner), jnp.bfloat16)] * 2
        + [jax.ShapeDtypeStruct((1, count), jnp.int32)],
        in_specs=[pl.BlockSpec(memory_space=pltpu.SMEM)] + [pl.BlockSpec(memory_space=pltpu.VMEM)] * 2,
        out_specs=[pl.BlockSpec(memory_space=pltpu.VMEM)] * 3,
        cost_estimate=pl.CostEstimate(flops=0, bytes_accessed=4 * tiles.size, transcendentals=0),
        compiler_params=pltpu.CompilerParams(vmem_limit_bytes=8 * 1024 * 1024),
    )(core, tile_row.reshape(1, count), tiles)

    def row_sums(turned):
        return pl.pallas_call(
            sum_kernel,
            out_shape=jax.ShapeDtypeStruct((rows_local, half, block), jnp.float32),
            in_specs=[pl.BlockSpec(memory_space=pltpu.VMEM)] * 3,
            out_specs=pl.BlockSpec(memory_space=pltpu.VMEM),
            scratch_shapes=[
                pltpu.SMEM((1, count), jnp.int32),
                pltpu.VMEM((count, half, block), jnp.float32),
                pltpu.SemaphoreType.DMA,
            ],
            cost_estimate=pl.CostEstimate(
                flops=2 * tiles.size * half, bytes_accessed=4 * tiles.size, transcendentals=0
            ),
            compiler_params=pltpu.CompilerParams(vmem_limit_bytes=16 * 1024 * 1024),
        )(near_row, turned, panels)

    other = lax.ppermute(row_sums(sent), "aux", [(0, 1), (1, 0)])
    return row_sums(kept) + other


def solution(mesh):
    orbs, grps, cores = mesh.devices.shape
    split = Mesh(mesh.devices.reshape(orbs, grps // Z, Z, cores), ("orb", "x", "z", "aux"))
    own = ("orb", "x", "z")
    return jax.shard_map(
        shards,
        mesh=split,
        in_specs=(
            P(own, "aux", None),
            P(own, None),
            P(own),
            P(own),
            P("orb", ("x", "z"), "aux", None),
        ),
        out_specs=P(own, "aux", None),
        check_vma=False,
    )
```

time: 91.6 us -> 88.7 us (0.968)
  waiting for transfers between devices: 16.5 us -> 14 us
  local copies, waits for them, and re-layouts: 2.84 us -> 1.66 us
    all_to_all x1, waiting for transfers between devices: 15.2 us -> 13.4 us  [shards(): lax.all_to_all(picked.reshape(plane, count * part, block), PLANE, 0, 0, t...]
    pallas_call x1 -> x3, Pallas kernels: 1.32 us -> 2.58 us  [the longest x2 1.5 us: row_sums(): pl.pallas_call(sum_kernel, out_shape=jax.ShapeDtypeStruct((rows_local, ha...]
  transfers between devices with their start and end apart: 2 -> 2, of which waited for: 2 -> 2; matrix products, arithmetic and copies ran while one was open for 0% -> 0% of each run, Pallas kernels for 0% -> 2%
where the time goes in v3:
time: 88.7 us; the launch traced here: 88.4 us
  blocking collectives  51.4 us (58%)
  starting transfers between devices  15.3 us (17%)
  waiting for transfers between devices  14 us (16%)
  Pallas kernels  4.92 us (6%)
  local copies, waits for them, and re-layouts  1.66 us (2%)
  other arithmetic  0.93 us (1%)
    all_gather x1, blocking collectives, shards(): table = lax.all_gather(mine, 'z', axis=0, tiled=False)  31.8 us
    all_to_all x1, blocking collectives, shards(): inbound = lax.all_to_all(outbound, PLANE, 0, 0, tiled=True)  19.6 us
    all_to_all x1, waiting for transfers between devices, shards(): lax.all_to_all(picked.reshape(plane, count * part, block), PLANE, 0, 0, t...  13.4 us
    ppermute x1, starting transfers between devices, shards(): other = lax.ppermute(row_sums(sent), 'aux', [(0, 1), (1, 0)])  11.1 us
    all_to_all x1, starting transfers between devices, shards(): lax.all_to_all(picked.reshape(plane, count * part, block), PLANE, 0, 0, t...  4.25 us
    pallas_call x1, Pallas kernels, shards(): pl.pallas_call(pick_kernel, out_shape=jax.ShapeDtypeStruct((plane * count...  2.34 us
  transfers between devices with their start and end apart: 2, of which 2 were waited for; matrix products, arithmetic and copies ran while one was open for 0% of the time, Pallas kernels for 2%

profile of v3, /device:TPU:1, one launch (start us, length us, event | category | flops | bytes accessed | tf_op | source)
XLA Modules:
  0.0 88.4 jit_solution(7111583702783339355)
XLA Ops:
  0.0 0.0 copy-start.2
  0.0 0.0 copy-start.3
  0.0 0.9 %copy.7 = bf16[4,32,2,128]{3,2,0,1:T(2,128)(2,1)S(1)} copy(bf16[4,32,2,128]{3,2,1,0:T(2,128)(2,1)} %bitcast.41) | data formatting | bytes 131072 | tf_op jit(solution)/shard_map/reshape | solution.py:75
  0.9 0.0 copy-done.2
  0.9 0.0 copy-done.3
  1.0 19.6 %all_to_all.10 = bf16[32,16,128]{2,1,0:T(8,128)(2,1)S(1)} all-to-all(bf16[32,16,128]{2,1,0:T(8,128)(2,1)S(1)} %pad_maximum_fusion), channel_id=1, replica_groups=mesh['orb'=8,'x'=4,'z'=12,'aux'=2] {'orb','x'}, dimensions={0} | all-to-all | bytes 262144 | tf_op jit(solution)/shard_map/all_to_all | solution.py:77
  20.7 0.1 fusion
  20.8 0.1 add.35.index_hbm
  20.9 31.8 %all-gather = bf16[384,8,128]{2,1,0:T(8,128)(2,1)S(1)} all-gather(bf16[32,8,128]{2,1,0:T(8,128)(2,1)S(1)} %slice.19), channel_id=2, replica_groups=mesh['orb'=8,'x'=4,'z'=12,'aux'=2] {'z'}, dimensions={0}, use_global_device_ids=true | all-gather | bytes 851968 | tf_op jit(solution)/shard_map/all_gather | solution.py:81
  52.6 2.3 %shard_map.56 = bf16[1536,2,128]{2,1,0:T(2,128)(2,1)} custom-call(s32[12,128]{1,0:T(8,128)S(1)} %add.35.index_hbm, bf16[1536,2,128]{2,1,0:T(2,128)(2,1)S(1)} %bitcast.38), custom_call_target="tpu_custom_call" | custom-call | tf_op jit(solution)/shard_map/pallas_call | solution.py:83
  55.0 0.0 copy-start
  55.0 4.2 %all-to-all-start.1 = ((bf16[32,96,128]{2,1,0:T(8,128)(2,1)}), bf16[32,96,128]{2,1,0:T(8,128)(2,1)S(1)}, u32[]{:S(2)}, u32[]{:S(2)}) async-start(bf16[32,96,128]{2,1,0:T(8,128)(2,1)} %bitcast.11), calls=%async_computation.1 | async-start | bytes 1572864 | tf_op jit(solution)/shard_map/all_to_all | solution.py:96
  59.2 0.0 copy-start.1
  59.2 0.0 copy-done
  59.2 0.6 copy-done.1
  59.9 1.1 %shard_map.55 = (bf16[48,64,64]{2,1,0:T(8,128)(2,1)S(1)}, bf16[48,64,64]{2,1,0:T(8,128)(2,1)S(1)}, s32[1,48]{1,0:T(1,128)S(1)}) custom-call(s32[1]{0:T(128)} %bitcast.core_ref, s32[1,48]{1,0:T(1,128)S(1)} %bitcast.39, bf16[48,64,128]{2,1,0:T(8,128)(2,1)S(1)} %copy-done), custom_call_target="tpu_custom_call" | custom-call | bytes 1572864 | tf_op jit(solution)/shard_map/pallas_call | solution.py:100
  61.0 13.4 %all-to-all-done.1 = bf16[32,96,128]{2,1,0:T(8,128)(2,1)S(1)} async-done(((bf16[32,96,128]{2,1,0:T(8,128)(2,1)}), bf16[32,96,128]{2,1,0:T(8,128)(2,1)S(1)}, u32[]{:S(2)}, u32[]{:S(2)}) %all-to-all-start.1) | async-done | bytes 786464 | tf_op jit(solution)/shard_map/all_to_all | solution.py:96
  74.4 0.7 shard_map.58
  75.2 11.1 %collective-permute-start = (f32[12,64,128]{2,1,0:T(8,128)S(1)}, f32[12,64,128]{2,1,0:T(8,128)S(1)}, u32[]{:S(2)}, u32[]{:S(2)}) collective-permute-start(f32[12,64,128]{2,1,0:T(8,128)S(1)} %shard_map.58), channel_id=1, source_target_pairs={{0,1},{1,0},{2,3},{3,2},{4,5},{5,4},{6,7},{7,6},{8,9},{9,8},{10,11... | collective-permute-start | bytes 1179656 | tf_op jit(solution)/shard_map/ppermute | solution.py:127
  86.3 0.8 shard_map.57
  87.0 0.6 collective-permute-done
  87.6 0.8 add.36
  (6 shorter events, 0.1 us)
Async XLA Ops:
  0.0 0.9 %copy-start.2 = (s32[48]{0:T(128)S(1)}, s32[48]{0:T(128)}, u32[]{:S(2)}) copy-start(s32[48]{0:T(128)} %param.7) | copy-start | bytes 580
  0.0 0.9 %copy-start.3 = (s32[48,1]{0,1:T(1,128)S(1)}, s32[48,1]{0,1:T(1,128)}, u32[]{:S(2)}) copy-start(s32[48,1]{0,1:T(1,128)} %param.6) | copy-start | bytes 580
  55.0 4.3 %copy-start = (bf16[48,64,128]{2,1,0:T(8,128)(2,1)S(1)}, bf16[48,64,128]{2,1,0:T(8,128)(2,1)}, u32[]{:S(2)}) copy-start(bf16[48,64,128]{2,1,0:T(8,128)(2,1)} %tiles_ref.1) | copy-start | bytes 2359300
  55.0 19.5 %all-to-all-start.1 = ((bf16[32,96,128]{2,1,0:T(8,128)(2,1)}), bf16[32,96,128]{2,1,0:T(8,128)(2,1)S(1)}, u32[]{:S(2)}, u32[]{:S(2)}) async-start(bf16[32,96,128]{2,1,0:T(8,128)(2,1)} %bitcast.11), calls=%async_computation.1 | async-start | bytes 1572864 | tf_op jit(solution)/shard_map/all_to_all | solution.py:96
  59.2 0.7 copy-start.1
  75.2 12.4 %collective-permute-start = (f32[12,64,128]{2,1,0:T(8,128)S(1)}, f32[12,64,128]{2,1,0:T(8,128)S(1)}, u32[]{:S(2)}, u32[]{:S(2)}) collective-permute-start(f32[12,64,128]{2,1,0:T(8,128)S(1)} %shard_map.58), channel_id=1, source_target_pairs={{0,1},{1,0},{2,3},{3,2},{4,5},{5,4},{6,7},{7,6},{8,9},{9,8},{10,11... | collective-permute-start | bytes 1179656 | tf_op jit(solution)/shard_map/ppermute | solution.py:127

commit v4 on v3

--- a/solution.py
+++ b/solution.py
@@ -7,6 +7,11 @@
 
 Z = 12
 PLANE = ("orb", "x")
+TURN = (4, 2)
+
+
+def numbered(orbs, xs):
+    return [[(i // xs + TURN[0]) % orbs * xs + (i + TURN[1]) % xs for i in range(orbs * xs)]]
 
 
 def pick_kernel(index_hbm, table_ref, out_hbm, index_ref, out_ref, in_sem, out_sem):
@@ -63,22 +68,23 @@
 
 def shards(tiles, tile_owner, tile_panel, tile_row, density):
     plane = lax.axis_size(PLANE)
-    xs = lax.axis_size("x")
+    orbs, xs = lax.axis_size("orb"), lax.axis_size("x")
+    order = numbered(orbs, xs)
     count, inner, block = tiles.shape
     held = density.shape[0]
     part = inner // plane
     rows_local = count // 4
     owners = tile_owner[:, 0]
-    high = (owners % Z) * lax.axis_size("orb") + tile_panel // held
-    low = (owners // Z) * held + tile_panel % held
+    high = (Z - 1 - owners % Z) * orbs + (tile_panel // held - TURN[0]) % orbs
+    low = (owners // Z - TURN[1]) % xs * held + tile_panel % held
     asked = jnp.pad(jnp.stack([high, low]).astype(jnp.bfloat16), ((0, 6), (0, block - count)))
     slices = density.reshape(held, plane, part, block).transpose(1, 0, 2, 3).reshape(plane, held * part, block)
     outbound = jnp.concatenate([slices, jnp.broadcast_to(asked[None], (plane, 8, block))], axis=1)
-    inbound = lax.all_to_all(outbound, PLANE, 0, 0, tiled=True)
+    inbound = lax.all_to_all(outbound, PLANE, 0, 0, axis_index_groups=order, tiled=True)
     wanted = inbound[:, held * part : held * part + 2, :count].astype(jnp.int32)
     index = (wanted[:, 0] * (xs * held) + wanted[:, 1]).reshape(-1)
     mine = inbound[:, : held * part]
-    table = lax.all_gather(mine, "z", axis=0, tiled=False)
+    table = lax.all_gather(mine, "z", axis=0, axis_index_groups=[list(range(Z))[::-1]], tiled=False)
     pieces = 12
     picked = pl.pallas_call(
         pick_kernel,
@@ -93,7 +99,7 @@
         ],
         compiler_params=pltpu.CompilerParams(vmem_limit_bytes=16 * 1024 * 1024),
     )(index.reshape(-1, 128), table.reshape(Z * plane * held, part, block))
-    panels = lax.all_to_all(picked.reshape(plane, count * part, block), PLANE, 0, 0, tiled=True)
+    panels = lax.all_to_all(picked.reshape(plane, count * part, block), PLANE, 0, 0, axis_index_groups=order, tiled=True)
     panels = panels.reshape(plane, count, part, block)
     half = block // 2
     core = lax.axis_index("aux").reshape(1)

time: 88.7 us -> 82.6 us (0.931)
  blocking collectives: 51.4 us -> 45.4 us
  waiting for transfers between devices: 14 us -> 9.19 us
  starting transfers between devices: 15.3 us -> 20.1 us
    all_to_all x1, starting transfers between devices: 4.25 us -> 10.2 us  [shards(): lax.all_to_all(picked.reshape(plane, count * part, block), PLANE, 0, 0, a...]
    all_to_all x1, blocking collectives: 19.6 us -> 14.2 us  [shards(): lax.all_to_all(outbound, PLANE, 0, 0, axis_index_groups=order, tiled=True)]
    all_to_all x1, waiting for transfers between devices: 13.4 us -> 8.63 us  [shards(): lax.all_to_all(picked.reshape(plane, count * part, block), PLANE, 0, 0, a...]
    ppermute x1, starting transfers between devices: 11.1 us -> 9.86 us  [shards(): other = lax.ppermute(row_sums(sent), 'aux', [(0, 1), (1, 0)])]
where the time goes in v4:
time: 82.6 us; the launch traced here: 82.3 us
  blocking collectives  45.4 us (55%)
  starting transfers between devices  20.1 us (24%)
  waiting for transfers between devices  9.19 us (11%)
  Pallas kernels  4.93 us (6%)
  local copies, waits for them, and re-layouts  1.66 us (2%)
  other arithmetic  0.93 us (1%)
    all_gather x1, blocking collectives, shards(): lax.all_gather(mine, 'z', axis=0, axis_index_groups=[list(range(Z))[::-1]...  31.2 us
    all_to_all x1, blocking collectives, shards(): lax.all_to_all(outbound, PLANE, 0, 0, axis_index_groups=order, tiled=True)  14.2 us
    all_to_all x1, starting transfers between devices, shards(): lax.all_to_all(picked.reshape(plane, count * part, block), PLANE, 0, 0, a...  10.2 us
    ppermute x1, starting transfers between devices, shards(): other = lax.ppermute(row_sums(sent), 'aux', [(0, 1), (1, 0)])  9.86 us
    all_to_all x1, waiting for transfers between devices, shards(): lax.all_to_all(picked.reshape(plane, count * part, block), PLANE, 0, 0, a...  8.63 us
    pallas_call x1, Pallas kernels, shards(): pl.pallas_call(pick_kernel, out_shape=jax.ShapeDtypeStruct((plane * count...  2.34 us
  transfers between devices with their start and end apart: 2, of which 2 were waited for; matrix products, arithmetic and copies ran while one was open for 0% of the time, Pallas kernels for 2%

profile of v4, /device:TPU:1, one launch (start us, length us, event | category | flops | bytes accessed | tf_op | source)
XLA Modules:
  0.0 82.3 jit_solution(6999023647887075780)
XLA Ops:
  0.0 0.0 copy-start.2
  0.0 0.0 copy-start.3
  0.0 0.9 %copy.7 = bf16[4,32,2,128]{3,2,0,1:T(2,128)(2,1)S(1)} copy(bf16[4,32,2,128]{3,2,1,0:T(2,128)(2,1)} %bitcast.41) | data formatting | bytes 131072 | tf_op jit(solution)/shard_map/reshape | solution.py:81
  0.9 0.0 copy-done.2
  0.9 0.0 copy-done.3
  1.0 14.2 %all_to_all.10 = bf16[32,16,128]{2,1,0:T(8,128)(2,1)S(1)} all-to-all(bf16[32,16,128]{2,1,0:T(8,128)(2,1)S(1)} %pad_maximum_fusion), channel_id=1, replica_groups={{432,456,384,408,528,552,480,504,624,648,576,600,720,744,672,696,48,72,..., dimensions={0} | all-to-all | bytes 262144 | tf_op jit(solution)/shard_map/all_to_all | solution.py:83
  15.2 0.1 fusion
  15.3 0.1 add.47.index_hbm
  15.4 31.2 %all-gather = bf16[384,8,128]{2,1,0:T(8,128)(2,1)S(1)} all-gather(bf16[32,8,128]{2,1,0:T(8,128)(2,1)S(1)} %slice.19), channel_id=2, replica_groups={{22,20,18,16,14,12,10,8,6,4,2,0},{23,21,19,17,15,13,11,9,7,5,3,1},{46,4..., dimensions={0}, use_global_device_ids=true | all-gather | bytes 851968 | tf_op jit(solution)/shard_map/all_gather | solution.py:87
  46.6 2.3 %shard_map.56 = bf16[1536,2,128]{2,1,0:T(2,128)(2,1)} custom-call(s32[12,128]{1,0:T(8,128)S(1)} %add.47.index_hbm, bf16[1536,2,128]{2,1,0:T(2,128)(2,1)S(1)} %bitcast.38), custom_call_target="tpu_custom_call" | custom-call | tf_op jit(solution)/shard_map/pallas_call | solution.py:89
  49.0 0.0 copy-start
  49.0 10.2 %all-to-all-start.1 = ((bf16[32,96,128]{2,1,0:T(8,128)(2,1)}), bf16[32,96,128]{2,1,0:T(8,128)(2,1)S(1)}, u32[]{:S(2)}, u32[]{:S(2)}) async-start(bf16[32,96,128]{2,1,0:T(8,128)(2,1)} %bitcast.11), calls=%async_computation.1 | async-start | bytes 1572864 | tf_op jit(solution)/shard_map/all_to_all | solution.py:102
  59.2 0.0 copy-start.1
  59.2 0.0 copy-done
  59.2 0.6 copy-done.1
  59.8 1.1 %shard_map.55 = (bf16[48,64,64]{2,1,0:T(8,128)(2,1)S(1)}, bf16[48,64,64]{2,1,0:T(8,128)(2,1)S(1)}, s32[1,48]{1,0:T(1,128)S(1)}) custom-call(s32[1]{0:T(128)} %bitcast.core_ref, s32[1,48]{1,0:T(1,128)S(1)} %bitcast.39, bf16[48,64,128]{2,1,0:T(8,128)(2,1)S(1)} %copy-done), custom_call_target="tpu_custom_call" | custom-call | bytes 1572864 | tf_op jit(solution)/shard_map/pallas_call | solution.py:106
  60.9 8.6 %all-to-all-done.1 = bf16[32,96,128]{2,1,0:T(8,128)(2,1)S(1)} async-done(((bf16[32,96,128]{2,1,0:T(8,128)(2,1)}), bf16[32,96,128]{2,1,0:T(8,128)(2,1)S(1)}, u32[]{:S(2)}, u32[]{:S(2)}) %all-to-all-start.1) | async-done | bytes 786464 | tf_op jit(solution)/shard_map/all_to_all | solution.py:102
  69.6 0.8 shard_map.58
  70.3 9.9 %collective-permute-start = (f32[12,64,128]{2,1,0:T(8,128)S(1)}, f32[12,64,128]{2,1,0:T(8,128)S(1)}, u32[]{:S(2)}, u32[]{:S(2)}) collective-permute-start(f32[12,64,128]{2,1,0:T(8,128)S(1)} %shard_map.58), channel_id=1, source_target_pairs={{0,1},{1,0},{2,3},{3,2},{4,5},{5,4},{6,7},{7,6},{8,9},{9,8},{10,11... | collective-permute-start | bytes 1179656 | tf_op jit(solution)/shard_map/ppermute | solution.py:133
  80.2 0.8 shard_map.57
  81.0 0.6 collective-permute-done
  81.5 0.8 add.48
  (6 shorter events, 0.1 us)
Async XLA Ops:
  0.0 0.9 %copy-start.2 = (s32[48]{0:T(128)S(1)}, s32[48]{0:T(128)}, u32[]{:S(2)}) copy-start(s32[48]{0:T(128)} %param.7) | copy-start | bytes 580
  0.0 0.9 %copy-start.3 = (s32[48,1]{0,1:T(1,128)S(1)}, s32[48,1]{0,1:T(1,128)}, u32[]{:S(2)}) copy-start(s32[48,1]{0,1:T(1,128)} %param.6) | copy-start | bytes 580
  49.0 10.2 %copy-start = (bf16[48,64,128]{2,1,0:T(8,128)(2,1)S(1)}, bf16[48,64,128]{2,1,0:T(8,128)(2,1)}, u32[]{:S(2)}) copy-start(bf16[48,64,128]{2,1,0:T(8,128)(2,1)} %tiles_ref.1) | copy-start | bytes 2359300
  49.0 20.6 %all-to-all-start.1 = ((bf16[32,96,128]{2,1,0:T(8,128)(2,1)}), bf16[32,96,128]{2,1,0:T(8,128)(2,1)S(1)}, u32[]{:S(2)}, u32[]{:S(2)}) async-start(bf16[32,96,128]{2,1,0:T(8,128)(2,1)} %bitcast.11), calls=%async_computation.1 | async-start | bytes 1572864 | tf_op jit(solution)/shard_map/all_to_all | solution.py:102
  59.2 0.7 copy-start.1
  70.3 11.2 %collective-permute-start = (f32[12,64,128]{2,1,0:T(8,128)S(1)}, f32[12,64,128]{2,1,0:T(8,128)S(1)}, u32[]{:S(2)}, u32[]{:S(2)}) collective-permute-start(f32[12,64,128]{2,1,0:T(8,128)S(1)} %shard_map.58), channel_id=1, source_target_pairs={{0,1},{1,0},{2,3},{3,2},{4,5},{5,4},{6,7},{7,6},{8,9},{9,8},{10,11... | collective-permute-start | bytes 1179656 | tf_op jit(solution)/shard_map/ppermute | solution.py:133

commit v5 on v4

--- a/solution.py
+++ b/solution.py
@@ -14,27 +14,33 @@
     return [[(i // xs + TURN[0]) % orbs * xs + (i + TURN[1]) % xs for i in range(orbs * xs)]]
 
 
+IN_PARTS = (1, 3, 8)
+OUT_PARTS = (5, 4, 2, 1)
+
+
+def spans(lines, parts):
+    edges = [lines * sum(parts[:i]) // sum(parts) for i in range(len(parts) + 1)]
+    return list(zip(edges[:-1], edges[1:]))
+
+
 def pick_kernel(index_hbm, table_ref, out_hbm, index_ref, out_ref, in_sem, out_sem):
-    pieces = in_sem.shape[0]
     lines, width = index_ref.shape
-    per = lines // pieces
-    fetches, sends = [], []
-    for piece in range(pieces):
-        span = pl.ds(piece * per, per)
-        fetches.append(pltpu.make_async_copy(index_hbm.at[span], index_ref.at[span], in_sem.at[piece]))
-        fetches[-1].start()
-    for piece in range(pieces):
-        fetches[piece].wait()
-
-        def body(line, carry):
-            for i in range(width):
-                out_ref[line * width + i] = table_ref[index_ref[line, i]]
-            return carry
-
-        lax.fori_loop(piece * per, (piece + 1) * per, body, 0)
-        span = pl.ds(piece * per * width, per * width)
-        sends.append(pltpu.make_async_copy(out_ref.at[span], out_hbm.at[span], out_sem.at[piece]))
-        sends[-1].start()
+    fetches, sends = {}, []
+    for piece, (start, stop) in enumerate(spans(lines, IN_PARTS)):
+        span = pl.ds(start, stop - start)
+        fetches[start] = pltpu.make_async_copy(index_hbm.at[span], index_ref.at[span], in_sem.at[piece])
+        fetches[start].start()
+    outs = spans(lines, OUT_PARTS)
+    for line in range(lines):
+        if line in fetches:
+            fetches[line].wait()
+        for i in range(width):
+            out_ref[line * width + i] = table_ref[index_ref[line, i]]
+        if line + 1 == outs[len(sends)][1]:
+            start = outs[len(sends)][0] * width
+            span = pl.ds(start, (line + 1) * width - start)
+            sends.append(pltpu.make_async_copy(out_ref.at[span], out_hbm.at[span], out_sem.at[len(sends)]))
+            sends[-1].start()
     for send in sends:
         send.wait()
 
@@ -85,7 +91,6 @@
     index = (wanted[:, 0] * (xs * held) + wanted[:, 1]).reshape(-1)
     mine = inbound[:, : held * part]
     table = lax.all_gather(mine, "z", axis=0, axis_index_groups=[list(range(Z))[::-1]], tiled=False)
-    pieces = 12
     picked = pl.pallas_call(
         pick_kernel,
         out_shape=jax.ShapeDtypeStruct((plane * count, part, block), jnp.bfloat16),
@@ -94,8 +99,8 @@
         scratch_shapes=[
             pltpu.SMEM((plane * count // 128, 128), jnp.int32),
             pltpu.VMEM((plane * count, part, block), jnp.bfloat16),
-            pltpu.SemaphoreType.DMA((pieces,)),
-            pltpu.SemaphoreType.DMA((pieces,)),
+            pltpu.SemaphoreType.DMA((len(IN_PARTS),)),
+            pltpu.SemaphoreType.DMA((len(OUT_PARTS),)),
         ],
         compiler_params=pltpu.CompilerParams(vmem_limit_bytes=16 * 1024 * 1024),
     )(index.reshape(-1, 128), table.reshape(Z * plane * held, part, block))

time: 82.6 us -> 82.4 us (level)
  no operation moved by 1% of the time
where the time goes in v5:
time: 82.4 us; the launch traced here: 82.1 us
  blocking collectives  45.4 us (55%)
  starting transfers between devices  20.1 us (24%)
  waiting for transfers between devices  9.19 us (11%)
  Pallas kernels  4.67 us (6%)
  local copies, waits for them, and re-layouts  1.66 us (2%)
  other arithmetic  0.93 us (1%)
    all_gather x1, blocking collectives, shards(): lax.all_gather(mine, 'z', axis=0, axis_index_groups=[list(range(Z))[::-1]...  31.2 us
    all_to_all x1, blocking collectives, shards(): lax.all_to_all(outbound, PLANE, 0, 0, axis_index_groups=order, tiled=True)  14.2 us
    all_to_all x1, starting transfers between devices, shards(): lax.all_to_all(picked.reshape(plane, count * part, block), PLANE, 0, 0, a...  10.2 us
    ppermute x1, starting transfers between devices, shards(): other = lax.ppermute(row_sums(sent), 'aux', [(0, 1), (1, 0)])  9.86 us
    all_to_all x1, waiting for transfers between devices, shards(): lax.all_to_all(picked.reshape(plane, count * part, block), PLANE, 0, 0, a...  8.63 us
    pallas_call x1, Pallas kernels, shards(): pl.pallas_call(pick_kernel, out_shape=jax.ShapeDtypeStruct((plane * count...  2.07 us
  transfers between devices with their start and end apart: 2, of which 2 were waited for; matrix products, arithmetic and copies ran while one was open for 0% of the time, Pallas kernels for 2%

profile of v5, /device:TPU:1, one launch (start us, length us, event | category | flops | bytes accessed | tf_op | source)
XLA Modules:
  0.0 82.1 jit_solution(17885938058297931331)
XLA Ops:
  0.0 0.0 copy-start.2
  0.0 0.0 copy-start.3
  0.0 0.9 %copy.7 = bf16[4,32,2,128]{3,2,0,1:T(2,128)(2,1)S(1)} copy(bf16[4,32,2,128]{3,2,1,0:T(2,128)(2,1)} %bitcast.41) | data formatting | bytes 131072 | tf_op jit(solution)/shard_map/reshape | solution.py:87
  0.9 0.0 copy-done.2
  0.9 0.0 copy-done.3
  1.0 14.2 %all_to_all.10 = bf16[32,16,128]{2,1,0:T(8,128)(2,1)S(1)} all-to-all(bf16[32,16,128]{2,1,0:T(8,128)(2,1)S(1)} %pad_maximum_fusion), channel_id=1, replica_groups={{432,456,384,408,528,552,480,504,624,648,576,600,720,744,672,696,48,72,..., dimensions={0} | all-to-all | bytes 262144 | tf_op jit(solution)/shard_map/all_to_all | solution.py:89
  15.2 0.1 fusion
  15.3 0.1 add.47.index_hbm
  15.4 31.2 %all-gather = bf16[384,8,128]{2,1,0:T(8,128)(2,1)S(1)} all-gather(bf16[32,8,128]{2,1,0:T(8,128)(2,1)S(1)} %slice.19), channel_id=2, replica_groups={{22,20,18,16,14,12,10,8,6,4,2,0},{23,21,19,17,15,13,11,9,7,5,3,1},{46,4..., dimensions={0}, use_global_device_ids=true | all-gather | bytes 851968 | tf_op jit(solution)/shard_map/all_gather | solution.py:93
  46.6 2.1 %shard_map.56 = bf16[1536,2,128]{2,1,0:T(2,128)(2,1)} custom-call(s32[12,128]{1,0:T(8,128)S(1)} %add.47.index_hbm, bf16[1536,2,128]{2,1,0:T(2,128)(2,1)S(1)} %bitcast.38), custom_call_target="tpu_custom_call" | custom-call | tf_op jit(solution)/shard_map/pallas_call | solution.py:94
  48.7 0.0 copy-start
  48.7 10.2 %all-to-all-start.1 = ((bf16[32,96,128]{2,1,0:T(8,128)(2,1)}), bf16[32,96,128]{2,1,0:T(8,128)(2,1)S(1)}, u32[]{:S(2)}, u32[]{:S(2)}) async-start(bf16[32,96,128]{2,1,0:T(8,128)(2,1)} %bitcast.11), calls=%async_computation.1 | async-start | bytes 1572864 | tf_op jit(solution)/shard_map/all_to_all | solution.py:107
  58.9 0.0 copy-start.1
  58.9 0.0 copy-done
  58.9 0.6 copy-done.1
  59.6 1.1 %shard_map.55 = (bf16[48,64,64]{2,1,0:T(8,128)(2,1)S(1)}, bf16[48,64,64]{2,1,0:T(8,128)(2,1)S(1)}, s32[1,48]{1,0:T(1,128)S(1)}) custom-call(s32[1]{0:T(128)} %bitcast.core_ref, s32[1,48]{1,0:T(1,128)S(1)} %bitcast.39, bf16[48,64,128]{2,1,0:T(8,128)(2,1)S(1)} %copy-done), custom_call_target="tpu_custom_call" | custom-call | bytes 1572864 | tf_op jit(solution)/shard_map/pallas_call | solution.py:111
  60.7 8.6 %all-to-all-done.1 = bf16[32,96,128]{2,1,0:T(8,128)(2,1)S(1)} async-done(((bf16[32,96,128]{2,1,0:T(8,128)(2,1)}), bf16[32,96,128]{2,1,0:T(8,128)(2,1)S(1)}, u32[]{:S(2)}, u32[]{:S(2)}) %all-to-all-start.1) | async-done | bytes 786464 | tf_op jit(solution)/shard_map/all_to_all | solution.py:107
  69.3 0.8 shard_map.58
  70.1 9.9 %collective-permute-start = (f32[12,64,128]{2,1,0:T(8,128)S(1)}, f32[12,64,128]{2,1,0:T(8,128)S(1)}, u32[]{:S(2)}, u32[]{:S(2)}) collective-permute-start(f32[12,64,128]{2,1,0:T(8,128)S(1)} %shard_map.58), channel_id=1, source_target_pairs={{0,1},{1,0},{2,3},{3,2},{4,5},{5,4},{6,7},{7,6},{8,9},{9,8},{10,11... | collective-permute-start | bytes 1179656 | tf_op jit(solution)/shard_map/ppermute | solution.py:138
  79.9 0.8 shard_map.57
  80.7 0.6 collective-permute-done
  81.3 0.8 add.48
  (6 shorter events, 0.1 us)
Async XLA Ops:
  0.0 0.9 %copy-start.2 = (s32[48]{0:T(128)S(1)}, s32[48]{0:T(128)}, u32[]{:S(2)}) copy-start(s32[48]{0:T(128)} %param.7) | copy-start | bytes 580
  0.0 0.9 %copy-start.3 = (s32[48,1]{0,1:T(1,128)S(1)}, s32[48,1]{0,1:T(1,128)}, u32[]{:S(2)}) copy-start(s32[48,1]{0,1:T(1,128)} %param.6) | copy-start | bytes 580
  48.7 10.2 %copy-start = (bf16[48,64,128]{2,1,0:T(8,128)(2,1)S(1)}, bf16[48,64,128]{2,1,0:T(8,128)(2,1)}, u32[]{:S(2)}) copy-start(bf16[48,64,128]{2,1,0:T(8,128)(2,1)} %tiles_ref.1) | copy-start | bytes 2359300
  48.7 20.6 %all-to-all-start.1 = ((bf16[32,96,128]{2,1,0:T(8,128)(2,1)}), bf16[32,96,128]{2,1,0:T(8,128)(2,1)S(1)}, u32[]{:S(2)}, u32[]{:S(2)}) async-start(bf16[32,96,128]{2,1,0:T(8,128)(2,1)} %bitcast.11), calls=%async_computation.1 | async-start | bytes 1572864 | tf_op jit(solution)/shard_map/all_to_all | solution.py:107
  58.9 0.7 copy-start.1
  70.1 11.2 %collective-permute-start = (f32[12,64,128]{2,1,0:T(8,128)S(1)}, f32[12,64,128]{2,1,0:T(8,128)S(1)}, u32[]{:S(2)}, u32[]{:S(2)}) collective-permute-start(f32[12,64,128]{2,1,0:T(8,128)S(1)} %shard_map.58), channel_id=1, source_target_pairs={{0,1},{1,0},{2,3},{3,2},{4,5},{5,4},{6,7},{7,6},{8,9},{9,8},{10,11... | collective-permute-start | bytes 1179656 | tf_op jit(solution)/shard_map/ppermute | solution.py:138

commit v6 on v5

--- a/solution.py
+++ b/solution.py
@@ -7,7 +7,7 @@
 
 Z = 12
 PLANE = ("orb", "x")
-TURN = (4, 2)
+TURN = (5, 2)
 
 
 def numbered(orbs, xs):
@@ -21,6 +21,9 @@
 def spans(lines, parts):
     edges = [lines * sum(parts[:i]) // sum(parts) for i in range(len(parts) + 1)]
     return list(zip(edges[:-1], edges[1:]))
+
+
+ORDER2 = [[(4 + i // 4) % 8 * 4 + (2 + i) % 4 for i in range(32)]]
 
 
 def pick_kernel(index_hbm, table_ref, out_hbm, index_ref, out_ref, in_sem, out_sem):
@@ -88,6 +91,8 @@
     outbound = jnp.concatenate([slices, jnp.broadcast_to(asked[None], (plane, 8, block))], axis=1)
     inbound = lax.all_to_all(outbound, PLANE, 0, 0, axis_index_groups=order, tiled=True)
     wanted = inbound[:, held * part : held * part + 2, :count].astype(jnp.int32)
+    wanted = jnp.roll(wanted.reshape(8, 4, 2, count), 1, 0).reshape(32, 2, count)
+    tiles = jnp.roll(tiles.reshape(count, 8, 8, block), 1, 1).reshape(count, inner, block)
     index = (wanted[:, 0] * (xs * held) + wanted[:, 1]).reshape(-1)
     mine = inbound[:, : held * part]
     table = lax.all_gather(mine, "z", axis=0, axis_index_groups=[list(range(Z))[::-1]], tiled=False)
@@ -104,7 +109,7 @@
         ],
         compiler_params=pltpu.CompilerParams(vmem_limit_bytes=16 * 1024 * 1024),
     )(index.reshape(-1, 128), table.reshape(Z * plane * held, part, block))
-    panels = lax.all_to_all(picked.reshape(plane, count * part, block), PLANE, 0, 0, axis_index_groups=order, tiled=True)
+    panels = lax.all_to_all(picked.reshape(plane, count * part, block), PLANE, 0, 0, axis_index_groups=ORDER2, tiled=True)
     panels = panels.reshape(plane, count, part, block)
     half = block // 2
     core = lax.axis_index("aux").reshape(1)

time: 82.4 us -> 82.3 us (level)
  no operation moved by 1% of the time
where the time goes in v6:
time: 82.3 us; the launch traced here: 82 us
  blocking collectives  46.1 us (56%)
  starting transfers between devices  19.4 us (24%)
  waiting for transfers between devices  9.01 us (11%)
  Pallas kernels  4.66 us (6%)
  local copies, waits for them, and re-layouts  1.76 us (2%)
  other arithmetic  0.97 us (1%)
    all_gather x1, blocking collectives, shards(): lax.all_gather(mine, 'z', axis=0, axis_index_groups=[list(range(Z))[::-1]...  31.4 us
    all_to_all x1, blocking collectives, shards(): lax.all_to_all(outbound, PLANE, 0, 0, axis_index_groups=order, tiled=True)  14.6 us
    ppermute x1, starting transfers between devices, shards(): other = lax.ppermute(row_sums(sent), 'aux', [(0, 1), (1, 0)])  9.86 us
    all_to_all x1, starting transfers between devices, shards(): lax.all_to_all(picked.reshape(plane, count * part, block), PLANE, 0, 0, a...  9.49 us
    all_to_all x1, waiting for transfers between devices, shards(): lax.all_to_all(picked.reshape(plane, count * part, block), PLANE, 0, 0, a...  8.45 us
    pallas_call x1, Pallas kernels, shards(): pl.pallas_call(pick_kernel, out_shape=jax.ShapeDtypeStruct((plane * count...  2.07 us
  transfers between devices with their start and end apart: 2, of which 2 were waited for; matrix products, arithmetic and copies ran while one was open for 0% of the time, Pallas kernels for 2%

profile of v6, /device:TPU:1, one launch (start us, length us, event | category | flops | bytes accessed | tf_op | source)
XLA Modules:
  0.0 82.0 jit_solution(15730412071707148478)
XLA Ops:
  0.0 0.0 copy-start.2
  0.0 0.0 copy-start.3
  0.0 0.9 %copy.8 = bf16[4,32,2,128]{3,2,0,1:T(2,128)(2,1)S(1)} copy(bf16[4,32,2,128]{3,2,1,0:T(2,128)(2,1)} %bitcast.54) | data formatting | bytes 131072 | tf_op jit(solution)/shard_map/reshape | solution.py:90
  0.9 0.0 copy-done.2
  0.9 0.0 copy-done.3
  1.0 14.6 %all_to_all.10 = bf16[32,16,128]{2,1,0:T(8,128)(2,1)S(1)} all-to-all(bf16[32,16,128]{2,1,0:T(8,128)(2,1)S(1)} %pad_maximum_fusion), channel_id=1, replica_groups={{528,552,480,504,624,648,576,600,720,744,672,696,48,72,0,24,144,168,96,..., dimensions={0} | all-to-all | bytes 262144 | tf_op jit(solution)/shard_map/all_to_all | solution.py:92
  15.8 0.1 add.47.index_hbm
  15.8 31.4 %all-gather = bf16[384,8,128]{2,1,0:T(8,128)(2,1)S(1)} all-gather(bf16[32,8,128]{2,1,0:T(8,128)(2,1)S(1)} %slice.51), channel_id=2, replica_groups={{22,20,18,16,14,12,10,8,6,4,2,0},{23,21,19,17,15,13,11,9,7,5,3,1},{46,4..., dimensions={0}, use_global_device_ids=true | all-gather | bytes 851968 | tf_op jit(solution)/shard_map/all_gather | solution.py:98
  47.3 2.1 %shard_map.56 = bf16[1536,2,128]{2,1,0:T(2,128)(2,1)} custom-call(s32[12,128]{1,0:T(8,128)S(1)} %add.47.index_hbm, bf16[1536,2,128]{2,1,0:T(2,128)(2,1)S(1)} %bitcast.47), custom_call_target="tpu_custom_call" | custom-call | tf_op jit(solution)/shard_map/pallas_call | solution.py:99
  49.4 0.0 copy-start.1
  49.4 9.5 %all-to-all-start.1 = ((bf16[32,96,128]{2,1,0:T(8,128)(2,1)}), bf16[32,96,128]{2,1,0:T(8,128)(2,1)S(1)}, u32[]{:S(2)}, u32[]{:S(2)}) async-start(bf16[32,96,128]{2,1,0:T(8,128)(2,1)} %bitcast.16), calls=%async_computation.1 | async-start | bytes 1572864 | tf_op jit(solution)/shard_map/all_to_all | solution.py:112
  58.9 0.0 copy-done.1
  58.9 0.1 slice.45
  59.0 0.1 maximum_bitcast_fusion.tiles_ref
  59.1 0.0 copy-start
  59.1 0.6 copy-done
  59.7 1.1 %shard_map.55 = (bf16[48,64,64]{2,1,0:T(8,128)(2,1)S(1)}, bf16[48,64,64]{2,1,0:T(8,128)(2,1)S(1)}, s32[1,48]{1,0:T(1,128)S(1)}) custom-call(s32[1]{0:T(128)} %bitcast.core_ref, s32[1,48]{1,0:T(1,128)S(1)} %bitcast.48, bf16[48,64,128]{2,1,0:T(8,128)(2,1)S(1)} %maximum_bitcast_fusion.tiles_ref), custom_call_target="tpu_custom_call" | custom-call | bytes 1572864 | tf_op jit(solution)/shard_map/pallas_call | solution.py:116
  60.8 8.4 %all-to-all-done.1 = bf16[32,96,128]{2,1,0:T(8,128)(2,1)S(1)} async-done(((bf16[32,96,128]{2,1,0:T(8,128)(2,1)}), bf16[32,96,128]{2,1,0:T(8,128)(2,1)S(1)}, u32[]{:S(2)}, u32[]{:S(2)}) %all-to-all-start.1) | async-done | bytes 786464 | tf_op jit(solution)/shard_map/all_to_all | solution.py:112
  69.3 0.8 shard_map.58
  70.0 9.9 %collective-permute-start = (f32[12,64,128]{2,1,0:T(8,128)S(1)}, f32[12,64,128]{2,1,0:T(8,128)S(1)}, u32[]{:S(2)}, u32[]{:S(2)}) collective-permute-start(f32[12,64,128]{2,1,0:T(8,128)S(1)} %shard_map.58), channel_id=1, source_target_pairs={{0,1},{1,0},{2,3},{3,2},{4,5},{5,4},{6,7},{7,6},{8,9},{9,8},{10,11... | collective-permute-start | bytes 1179656 | tf_op jit(solution)/shard_map/ppermute | solution.py:143
  79.9 0.8 shard_map.57
  80.7 0.6 collective-permute-done
  81.2 0.8 add.48
  (12 shorter events, 0.2 us)
Async XLA Ops:
  0.0 0.9 %copy-start.2 = (s32[48]{0:T(128)S(1)}, s32[48]{0:T(128)}, u32[]{:S(2)}) copy-start(s32[48]{0:T(128)} %param.7) | copy-start | bytes 580
  0.0 0.9 %copy-start.3 = (s32[48,1]{0,1:T(1,128)S(1)}, s32[48,1]{0,1:T(1,128)}, u32[]{:S(2)}) copy-start(s32[48,1]{0,1:T(1,128)} %param.6) | copy-start | bytes 580
  49.4 9.5 %copy-start.1 = (bf16[48,64,128]{2,1,0:T(8,128)(2,1)S(1)}, bf16[48,64,128]{2,1,0:T(8,128)(2,1)}, u32[]{:S(2)}) copy-start(bf16[48,64,128]{2,1,0:T(8,128)(2,1)} %param.5) | copy-start | bytes 2359300
  49.4 19.9 %all-to-all-start.1 = ((bf16[32,96,128]{2,1,0:T(8,128)(2,1)}), bf16[32,96,128]{2,1,0:T(8,128)(2,1)S(1)}, u32[]{:S(2)}, u32[]{:S(2)}) async-start(bf16[32,96,128]{2,1,0:T(8,128)(2,1)} %bitcast.16), calls=%async_computation.1 | async-start | bytes 1572864 | tf_op jit(solution)/shard_map/all_to_all | solution.py:112
  59.1 0.7 copy-start
  70.0 11.2 %collective-permute-start = (f32[12,64,128]{2,1,0:T(8,128)S(1)}, f32[12,64,128]{2,1,0:T(8,128)S(1)}, u32[]{:S(2)}, u32[]{:S(2)}) collective-permute-start(f32[12,64,128]{2,1,0:T(8,128)S(1)} %shard_map.58), channel_id=1, source_target_pairs={{0,1},{1,0},{2,3},{3,2},{4,5},{5,4},{6,7},{7,6},{8,9},{9,8},{10,11... | collective-permute-start | bytes 1179656 | tf_op jit(solution)/shard_map/ppermute | solution.py:143

commit v7 on v6

--- a/solution.py
+++ b/solution.py
@@ -86,9 +86,9 @@
     owners = tile_owner[:, 0]
     high = (Z - 1 - owners % Z) * orbs + (tile_panel // held - TURN[0]) % orbs
     low = (owners // Z - TURN[1]) % xs * held + tile_panel % held
-    asked = jnp.pad(jnp.stack([high, low]).astype(jnp.bfloat16), ((0, 6), (0, block - count)))
+    asked = jnp.pad(jnp.stack([high, low]).astype(jnp.bfloat16), ((0, 0), (0, block - count)))
     slices = density.reshape(held, plane, part, block).transpose(1, 0, 2, 3).reshape(plane, held * part, block)
-    outbound = jnp.concatenate([slices, jnp.broadcast_to(asked[None], (plane, 8, block))], axis=1)
+    outbound = jnp.concatenate([slices, jnp.broadcast_to(asked[None], (plane, 2, block))], axis=1)
     inbound = lax.all_to_all(outbound, PLANE, 0, 0, axis_index_groups=order, tiled=True)
     wanted = inbound[:, held * part : held * part + 2, :count].astype(jnp.int32)
     wanted = jnp.roll(wanted.reshape(8, 4, 2, count), 1, 0).reshape(32, 2, count)

time: 82.3 us -> 82.3 us (level)
  no operation moved by 1% of the time
where the time goes in v7:
time: 82.3 us; the launch traced here: 82 us
  blocking collectives  46.1 us (56%)
  starting transfers between devices  19.4 us (24%)
  waiting for transfers between devices  9.01 us (11%)
  Pallas kernels  4.66 us (6%)
  local copies, waits for them, and re-layouts  1.76 us (2%)
  other arithmetic  0.97 us (1%)
    all_gather x1, blocking collectives, shards(): lax.all_gather(mine, 'z', axis=0, axis_index_groups=[list(range(Z))[::-1]...  31.4 us
    all_to_all x1, blocking collectives, shards(): lax.all_to_all(outbound, PLANE, 0, 0, axis_index_groups=order, tiled=True)  14.6 us
    ppermute x1, starting transfers between devices, shards(): other = lax.ppermute(row_sums(sent), 'aux', [(0, 1), (1, 0)])  9.86 us
    all_to_all x1, starting transfers between devices, shards(): lax.all_to_all(picked.reshape(plane, count * part, block), PLANE, 0, 0, a...  9.49 us
    all_to_all x1, waiting for transfers between devices, shards(): lax.all_to_all(picked.reshape(plane, count * part, block), PLANE, 0, 0, a...  8.45 us
    pallas_call x1, Pallas kernels, shards(): pl.pallas_call(pick_kernel, out_shape=jax.ShapeDtypeStruct((plane * count...  2.07 us
  transfers between devices with their start and end apart: 2, of which 2 were waited for; matrix products, arithmetic and copies ran while one was open for 0% of the time, Pallas kernels for 2%

profile of v7, /device:TPU:1, one launch (start us, length us, event | category | flops | bytes accessed | tf_op | source)
XLA Modules:
  0.0 82.0 jit_solution(12550220244636185994)
XLA Ops:
  0.0 0.0 copy-start.2
  0.0 0.0 copy-start.3
  0.0 0.9 %copy.8 = bf16[4,32,2,128]{3,2,0,1:T(2,128)(2,1)S(1)} copy(bf16[4,32,2,128]{3,2,1,0:T(2,128)(2,1)} %bitcast.54) | data formatting | bytes 131072 | tf_op jit(solution)/shard_map/reshape | solution.py:90
  0.9 0.0 copy-done.2
  0.9 0.0 copy-done.3
  1.0 14.6 %all_to_all.10 = bf16[32,10,128]{2,1,0:T(8,128)(2,1)S(1)} all-to-all(bf16[32,10,128]{2,1,0:T(8,128)(2,1)S(1)} %pad_maximum_fusion), channel_id=1, replica_groups={{528,552,480,504,624,648,576,600,720,744,672,696,48,72,0,24,144,168,96,..., dimensions={0} | all-to-all | bytes 163840 | tf_op jit(solution)/shard_map/all_to_all | solution.py:92
  15.8 0.1 add.47.index_hbm
  15.9 31.4 %all-gather = bf16[384,8,128]{2,1,0:T(8,128)(2,1)S(1)} all-gather(bf16[32,8,128]{2,1,0:T(8,128)(2,1)S(1)} %slice.51), channel_id=2, replica_groups={{22,20,18,16,14,12,10,8,6,4,2,0},{23,21,19,17,15,13,11,9,7,5,3,1},{46,4..., dimensions={0}, use_global_device_ids=true | all-gather | bytes 851968 | tf_op jit(solution)/shard_map/all_gather | solution.py:98
  47.3 2.1 %shard_map.56 = bf16[1536,2,128]{2,1,0:T(2,128)(2,1)} custom-call(s32[12,128]{1,0:T(8,128)S(1)} %add.47.index_hbm, bf16[1536,2,128]{2,1,0:T(2,128)(2,1)S(1)} %bitcast.47), custom_call_target="tpu_custom_call" | custom-call | tf_op jit(solution)/shard_map/pallas_call | solution.py:99
  49.4 0.0 copy-start.1
  49.4 9.5 %all-to-all-start.1 = ((bf16[32,96,128]{2,1,0:T(8,128)(2,1)}), bf16[32,96,128]{2,1,0:T(8,128)(2,1)S(1)}, u32[]{:S(2)}, u32[]{:S(2)}) async-start(bf16[32,96,128]{2,1,0:T(8,128)(2,1)} %bitcast.16), calls=%async_computation.1 | async-start | bytes 1572864 | tf_op jit(solution)/shard_map/all_to_all | solution.py:112
  58.9 0.0 copy-done.1
  58.9 0.1 slice.45
  59.0 0.1 maximum_bitcast_fusion.tiles_ref
  59.1 0.0 copy-start
  59.1 0.6 copy-done
  59.7 1.1 %shard_map.55 = (bf16[48,64,64]{2,1,0:T(8,128)(2,1)S(1)}, bf16[48,64,64]{2,1,0:T(8,128)(2,1)S(1)}, s32[1,48]{1,0:T(1,128)S(1)}) custom-call(s32[1]{0:T(128)} %bitcast.core_ref, s32[1,48]{1,0:T(1,128)S(1)} %bitcast.48, bf16[48,64,128]{2,1,0:T(8,128)(2,1)S(1)} %maximum_bitcast_fusion.tiles_ref), custom_call_target="tpu_custom_call" | custom-call | bytes 1572864 | tf_op jit(solution)/shard_map/pallas_call | solution.py:116
  60.8 8.4 %all-to-all-done.1 = bf16[32,96,128]{2,1,0:T(8,128)(2,1)S(1)} async-done(((bf16[32,96,128]{2,1,0:T(8,128)(2,1)}), bf16[32,96,128]{2,1,0:T(8,128)(2,1)S(1)}, u32[]{:S(2)}, u32[]{:S(2)}) %all-to-all-start.1) | async-done | bytes 786464 | tf_op jit(solution)/shard_map/all_to_all | solution.py:112
  69.3 0.8 shard_map.58
  70.0 9.9 %collective-permute-start = (f32[12,64,128]{2,1,0:T(8,128)S(1)}, f32[12,64,128]{2,1,0:T(8,128)S(1)}, u32[]{:S(2)}, u32[]{:S(2)}) collective-permute-start(f32[12,64,128]{2,1,0:T(8,128)S(1)} %shard_map.58), channel_id=1, source_target_pairs={{0,1},{1,0},{2,3},{3,2},{4,5},{5,4},{6,7},{7,6},{8,9},{9,8},{10,11... | collective-permute-start | bytes 1179656 | tf_op jit(solution)/shard_map/ppermute | solution.py:143
  79.9 0.8 shard_map.57
  80.7 0.6 collective-permute-done
  81.2 0.8 add.48
  (12 shorter events, 0.2 us)
Async XLA Ops:
  0.0 0.9 %copy-start.2 = (s32[48]{0:T(128)S(1)}, s32[48]{0:T(128)}, u32[]{:S(2)}) copy-start(s32[48]{0:T(128)} %param.7) | copy-start | bytes 580
  0.0 0.9 %copy-start.3 = (s32[48,1]{0,1:T(1,128)S(1)}, s32[48,1]{0,1:T(1,128)}, u32[]{:S(2)}) copy-start(s32[48,1]{0,1:T(1,128)} %param.6) | copy-start | bytes 580
  49.4 9.5 %copy-start.1 = (bf16[48,64,128]{2,1,0:T(8,128)(2,1)S(1)}, bf16[48,64,128]{2,1,0:T(8,128)(2,1)}, u32[]{:S(2)}) copy-start(bf16[48,64,128]{2,1,0:T(8,128)(2,1)} %param.5) | copy-start | bytes 2359300
  49.4 19.9 %all-to-all-start.1 = ((bf16[32,96,128]{2,1,0:T(8,128)(2,1)}), bf16[32,96,128]{2,1,0:T(8,128)(2,1)S(1)}, u32[]{:S(2)}, u32[]{:S(2)}) async-start(bf16[32,96,128]{2,1,0:T(8,128)(2,1)} %bitcast.16), calls=%async_computation.1 | async-start | bytes 1572864 | tf_op jit(solution)/shard_map/all_to_all | solution.py:112
  59.1 0.7 copy-start
  70.0 11.2 %collective-permute-start = (f32[12,64,128]{2,1,0:T(8,128)S(1)}, f32[12,64,128]{2,1,0:T(8,128)S(1)}, u32[]{:S(2)}, u32[]{:S(2)}) collective-permute-start(f32[12,64,128]{2,1,0:T(8,128)S(1)} %shard_map.58), channel_id=1, source_target_pairs={{0,1},{1,0},{2,3},{3,2},{4,5},{5,4},{6,7},{7,6},{8,9},{9,8},{10,11... | collective-permute-start | bytes 1179656 | tf_op jit(solution)/shard_map/ppermute | solution.py:143
